TPU v7x, 512 devices: a whole 4x4x16 slice. The times are simulated.
512 devices in a mesh: tm: 32 (over z_lo, x), space: 16 (over y, z_hi, core).
Axes of the slice: x: 4, y: 4, z: 16 (z_hi: 2, z_lo: 8; z = z_hi * 8 + z_lo), core: 2. Of those that a mesh axis runs over, the one named last changes fastest.
Arguments:
- base_states: float32 [32, 2, 128, 128, 128], P('tm', None, 'space'), may hold values from 0 to 1
- direction: float32 [32, 2, 128, 128, 128], P('tm', None, 'space'), may hold values from -6 to 6
Outputs:
- product: float32 [32, 2, 128, 128, 128], P('tm', None, 'space')
All inputs are finite; a program needn't handle non-finite values.
Results may differ from a plain program's by a relative error of at most 0.00002.
Values sent between devices are 32-bit elements; how exact they have to be, the bound alone decides.
A program may use at most 64 MiB of HBM per device.

v0:
```python
import jax
import jax.numpy as jnp
from jax import lax
from jax.sharding import PartitionSpec as P

diff_substrate = 0.2
diff_catalyst = 0.1
time_step = 0.8
feed_rate = 0.04
kill_rate = 0.06


def from_behind(value, axis, steps):
    count = lax.axis_size(axis)
    pairs = [(source, (source + steps) % count) for source in range(count)]
    return lax.ppermute(value, axis, pairs)


def padded(array, sides, width):
    for axis, dim in sides:
        size, length = (lax.axis_size(axis), array.shape[dim])
        up = [(i, (i + 1) % size) for i in range(size)]
        down = [(j, i) for i, j in up]
        last = lax.slice_in_dim(array, length - width, length, axis=dim)
        initial = lax.slice_in_dim(array, 0, width, axis=dim)
        before = lax.ppermute(last, axis, up)
        after = lax.ppermute(initial, axis, down)
        array = jnp.concatenate([before, array, after], axis=dim)
    return array


def laplacian(extended):
    core_cells = extended[:, 1:-1]
    total = -6.0 * core_cells + extended[:, 2:] + extended[:, :-2]
    total = total + jnp.roll(core_cells, 1, 2) + jnp.roll(core_cells, -1, 2)
    return total + jnp.roll(core_cells, 1, 3) + jnp.roll(core_cells, -1, 3)


def base_advance(state, spread):
    substrate = state[0]
    catalyst = state[1]
    growth = substrate * catalyst * catalyst
    next_substrate = substrate + time_step * (
        diff_substrate * spread[0] - growth + feed_rate * (1.0 - substrate)
    )
    next_catalyst = catalyst + time_step * (
        diff_catalyst * spread[1] + growth - (feed_rate + kill_rate) * catalyst
    )
    return jnp.stack([next_substrate, next_catalyst])


def tangent_advance(state, tangent, spread):
    square = state[1] * state[1]
    cross = 2.0 * state[0] * state[1]
    next_substrate = tangent[0] + time_step * (
        diff_substrate * spread[0] - (square + feed_rate) * tangent[0] - cross * tangent[1]
    )
    next_catalyst = tangent[1] + time_step * (
        diff_catalyst * spread[1]
        + square * tangent[0]
        + (cross - feed_rate - kill_rate) * tangent[1]
    )
    return jnp.stack([next_substrate, next_catalyst])


def adjoint_advance(state, adjoint, spread):
    square = state[1] * state[1]
    cross = 2.0 * state[0] * state[1]
    next_substrate = adjoint[0] + time_step * (
        diff_substrate * spread[0] - (square + feed_rate) * adjoint[0] + square * adjoint[1]
    )
    next_catalyst = adjoint[1] + time_step * (
        diff_catalyst * spread[1]
        - cross * adjoint[0]
        + (cross - feed_rate - kill_rate) * adjoint[1]
    )
    return jnp.stack([next_substrate, next_catalyst])


def local(base_states, direction):
    state = base_states[0]
    tangent = direction[0]
    following = from_behind(tangent, "tm", -1)
    joined = jnp.concatenate([state, tangent])
    extended = padded(joined, (("space", 1),), 1)
    spread = laplacian(extended)
    later_state = base_advance(state, spread[:2])
    middle = tangent_advance(state, tangent, spread[2:])
    middle_ext = padded(middle, (("space", 1),), 1)
    image = tangent_advance(later_state, middle, laplacian(middle_ext))
    residual = image - following
    prior = from_behind(residual, "tm", 1)
    residual_ext = padded(residual, (("space", 1),), 1)
    adjoint_mid = adjoint_advance(later_state, residual, laplacian(residual_ext))
    adjoint_ext = padded(adjoint_mid, (("space", 1),), 1)
    pulled = adjoint_advance(state, adjoint_mid, laplacian(adjoint_ext))
    return (pulled - prior)[None]


def solution(mesh):
    return jax.shard_map(
        local,
        mesh=mesh,
        in_specs=(P("tm", None, "space", None, None), P("tm", None, "space", None, None)),
        out_specs=P("tm", None, "space", None, None),
        check_vma=False,
    )
```

profile of v0, /device:TPU:134, one launch (start us, length us, event | category | flops | bytes accessed | tf_op | source)
XLA Modules:
  0.0 160.4 jit_solution(1278345552642161857)
XLA Ops:
  0.0 0.0 copy-start.1
  0.0 0.0 copy-start
  0.0 2.9 %collective-permute-start.4 = (f32[2,8,128,128]{3,2,1,0:T(8,128)}, f32[2,8,128,128]{3,2,1,0:T(8,128)S(1)}, u32[]{:S(2)}, u32[]{:S(2)}) collective-permute-start(f32[2,8,128,128]{3,2,1,0:T(8,128)} %bitcast.71), channel_id=1, source_target_pairs={{0,496},{16,0},{32,16},{48,32},{64,48},{80,64},{96,80},{112,96},{1... | collective-permute-start | bytes 3145736 | tf_op jit(solution)/shard_map/ppermute | solution.py:16
  2.9 1.1 fusion.90
  4.0 12.5 %collective-permute-start = (f32[4,1,128,128]{3,2,1,0:T(8,128)S(1)}, f32[4,1,128,128]{3,2,1,0:T(8,128)S(1)}, u32[]{:S(2)}, u32[]{:S(2)}) collective-permute-start(f32[4,1,128,128]{3,2,1,0:T(8,128)S(1)} %get-tuple-element.22), channel_id=1, source_target_pairs={{1,0},{2,1},{3,2},{4,3},{5,4},{6,5},{7,6},{8,7},{9,8},{10,9},{11,1... | collective-permute-start | bytes 786440 | tf_op jit(solution)/shard_map/ppermute | solution.py:27
  16.5 1.9 %collective-permute-start.1 = (f32[4,1,128,128]{3,2,1,0:T(8,128)S(1)}, f32[4,1,128,128]{3,2,1,0:T(8,128)S(1)}, u32[]{:S(2)}, u32[]{:S(2)}) collective-permute-start(f32[4,1,128,128]{3,2,1,0:T(8,128)S(1)} %get-tuple-element.23), channel_id=1, source_target_pairs={{0,1},{1,2},{2,3},{3,4},{4,5},{5,6},{6,7},{7,8},{8,9},{9,10},{10,1... | collective-permute-start | bytes 786440 | tf_op jit(solution)/shard_map/ppermute | solution.py:26
  18.5 0.0 copy-done.1
  18.5 0.0 copy-done
  18.5 0.7 fusion.4
  19.3 0.8 fusion.5
  20.0 0.5 fusion.1
  20.6 9.2 %collective-permute-done = f32[4,1,128,128]{3,2,1,0:T(8,128)S(1)} collective-permute-done((f32[4,1,128,128]{3,2,1,0:T(8,128)S(1)}, f32[4,1,128,128]{3,2,1,0:T(8,128)S(1)}, u32[]{:S(2)}, u32[]{:S(2)}) %collective-permute-start) | collective-permute-done | bytes 262176 | tf_op jit(solution)/shard_map/ppermute | solution.py:27
  29.8 8.2 %collective-permute-done.1 = f32[4,1,128,128]{3,2,1,0:T(8,128)S(1)} collective-permute-done((f32[4,1,128,128]{3,2,1,0:T(8,128)S(1)}, f32[4,1,128,128]{3,2,1,0:T(8,128)S(1)}, u32[]{:S(2)}, u32[]{:S(2)}) %collective-permute-start.1) | collective-permute-done | bytes 262176 | tf_op jit(solution)/shard_map/ppermute | solution.py:26
  38.0 2.4 %fusion.12 = f32[4,8,128,128]{3,2,1,0:T(8,128)S(1)} fusion(f32[2,8,128,128]{3,2,1,0:T(8,128)S(1)} %bitcast.77, f32[2,8,128,128]{3,2,1,0:T(8,128)S(1)} %bitcast.70, f32[4,1,128,128]{3,2,1,0:T(8,128)S(1)} %collective-permute-done.1, f32[4,1,128,128]{3,2,1,0:T(8,128)S(1)} %collective-permute-done, f32[4,8,127,128]{3,2,1,0:T(8,128)S(1)} %get-tuple-element.19, ...), kind=kLoop, calls=%fused_computation.75 | loop fusion | flops 8388608 | bytes 13107200 | tf_op jit(solution)/shard_map/add | solution.py:36
  40.3 0.4 fusion.87
  40.7 0.4 fusion.31
  41.1 0.4 fusion.30
  41.5 6.8 %collective-permute-start.2 = (f32[2,1,128,128]{3,2,1,0:T(8,128)S(1)}, f32[2,1,128,128]{3,2,1,0:T(8,128)S(1)}, u32[]{:S(2)}, u32[]{:S(2)}) collective-permute-start(f32[2,1,128,128]{3,2,1,0:T(8,128)S(1)} %get-tuple-element.52), channel_id=1, source_target_pairs={{1,0},{2,1},{3,2},{4,3},{5,4},{6,5},{7,6},{8,7},{9,8},{10,9},{11,1... | collective-permute-start | bytes 393224 | tf_op jit(solution)/shard_map/ppermute | solution.py:27
  48.2 1.9 %collective-permute-start.3 = (f32[2,1,128,128]{3,2,1,0:T(8,128)S(1)}, f32[2,1,128,128]{3,2,1,0:T(8,128)S(1)}, u32[]{:S(2)}, u32[]{:S(2)}) collective-permute-start(f32[2,1,128,128]{3,2,1,0:T(8,128)S(1)} %get-tuple-element.53), channel_id=1, source_target_pairs={{0,1},{1,2},{2,3},{3,4},{4,5},{5,6},{6,7},{7,8},{8,9},{9,10},{10,1... | collective-permute-start | bytes 393224 | tf_op jit(solution)/shard_map/ppermute | solution.py:26
  50.1 0.2 fusion.27
  50.4 1.4 collective-permute-done.2
  51.8 13.7 %collective-permute-done.3 = f32[2,1,128,128]{3,2,1,0:T(8,128)S(1)} collective-permute-done((f32[2,1,128,128]{3,2,1,0:T(8,128)S(1)}, f32[2,1,128,128]{3,2,1,0:T(8,128)S(1)}, u32[]{:S(2)}, u32[]{:S(2)}) %collective-permute-start.3) | collective-permute-done | bytes 131104 | tf_op jit(solution)/shard_map/ppermute | solution.py:26
  65.5 1.0 fusion.38
  66.5 0.5 fusion.79
  67.0 0.2 fusion.65
  67.2 0.0 collective-permute-done.4
  67.2 0.1 maximum_subtract_fusion
  67.3 0.4 fusion.104
  67.7 0.4 fusion.105
  68.0 0.2 fusion.106
  68.3 24.5 %collective-permute-start.9 = (f32[2,8,128,128]{3,2,1,0:T(8,128)S(1)}, f32[2,8,128,128]{3,2,1,0:T(8,128)S(1)}, u32[]{:S(2)}, u32[]{:S(2)}) collective-permute-start(f32[2,8,128,128]{3,2,1,0:T(8,128)S(1)} %maximum_subtract_fusion), channel_id=1, source_target_pairs={{0,16},{16,32},{32,48},{48,64},{64,80},{80,96},{96,112},{112,128},... | collective-permute-start | bytes 3145736 | tf_op jit(solution)/shard_map/ppermute | solution.py:16
  92.8 1.9 %collective-permute-start.5 = (f32[2,1,128,128]{3,2,1,0:T(8,128)S(1)}, f32[2,1,128,128]{3,2,1,0:T(8,128)S(1)}, u32[]{:S(2)}, u32[]{:S(2)}) collective-permute-start(f32[2,1,128,128]{3,2,1,0:T(8,128)S(1)} %get-tuple-element.42), channel_id=1, source_target_pairs={{1,0},{2,1},{3,2},{4,3},{5,4},{6,5},{7,6},{8,7},{9,8},{10,9},{11,1... | collective-permute-start | bytes 393224 | tf_op jit(solution)/shard_map/ppermute | solution.py:27
  94.7 2.4 %collective-permute-start.6 = (f32[2,1,128,128]{3,2,1,0:T(8,128)S(1)}, f32[2,1,128,128]{3,2,1,0:T(8,128)S(1)}, u32[]{:S(2)}, u32[]{:S(2)}) collective-permute-start(f32[2,1,128,128]{3,2,1,0:T(8,128)S(1)} %get-tuple-element.43), channel_id=1, source_target_pairs={{0,1},{1,2},{2,3},{3,4},{4,5},{5,6},{6,7},{7,8},{8,9},{9,10},{10,1... | collective-permute-start | bytes 393224 | tf_op jit(solution)/shard_map/ppermute | solution.py:26
  97.1 27.5 %collective-permute-done.5 = f32[2,1,128,128]{3,2,1,0:T(8,128)S(1)} collective-permute-done((f32[2,1,128,128]{3,2,1,0:T(8,128)S(1)}, f32[2,1,128,128]{3,2,1,0:T(8,128)S(1)}, u32[]{:S(2)}, u32[]{:S(2)}) %collective-permute-start.5) | collective-permute-done | bytes 131104 | tf_op jit(solution)/shard_map/ppermute | solution.py:27
  124.7 0.0 collective-permute-done.6
  124.7 1.0 fusion.43
  125.6 0.4 fusion.61
  126.0 14.8 %collective-permute-start.7 = (f32[2,1,128,128]{3,2,1,0:T(8,128)S(1)}, f32[2,1,128,128]{3,2,1,0:T(8,128)S(1)}, u32[]{:S(2)}, u32[]{:S(2)}) collective-permute-start(f32[2,1,128,128]{3,2,1,0:T(8,128)S(1)} %get-tuple-element.32), channel_id=1, source_target_pairs={{1,0},{2,1},{3,2},{4,3},{5,4},{6,5},{7,6},{8,7},{9,8},{10,9},{11,1... | collective-permute-start | bytes 393224 | tf_op jit(solution)/shard_map/ppermute | solution.py:27
  140.8 1.9 %collective-permute-start.8 = (f32[2,1,128,128]{3,2,1,0:T(8,128)S(1)}, f32[2,1,128,128]{3,2,1,0:T(8,128)S(1)}, u32[]{:S(2)}, u32[]{:S(2)}) collective-permute-start(f32[2,1,128,128]{3,2,1,0:T(8,128)S(1)} %get-tuple-element.33), channel_id=1, source_target_pairs={{0,1},{1,2},{2,3},{3,4},{4,5},{5,6},{6,7},{7,8},{8,9},{9,10},{10,1... | collective-permute-start | bytes 393224 | tf_op jit(solution)/shard_map/ppermute | solution.py:26
  142.7 0.4 fusion.18
  143.1 0.4 fusion.17
  143.5 0.2 fusion.14
  143.7 0.2 collective-permute-done.7
  143.9 14.0 %collective-permute-done.8 = f32[2,1,128,128]{3,2,1,0:T(8,128)S(1)} collective-permute-done((f32[2,1,128,128]{3,2,1,0:T(8,128)S(1)}, f32[2,1,128,128]{3,2,1,0:T(8,128)S(1)}, u32[]{:S(2)}, u32[]{:S(2)}) %collective-permute-start.8) | collective-permute-done | bytes 131104 | tf_op jit(solution)/shard_map/ppermute | solution.py:26
  157.9 1.0 fusion.25
  158.9 0.4 fusion.53
  159.3 0.0 collective-permute-done.9
  159.3 1.1 fusion.45
  (7 shorter events, 0.1 us)
Async XLA Ops:
  0.0 18.5 %copy-start.1 = (f32[1,2,8,128,128]{4,3,2,1,0:T(8,128)S(1)}, f32[1,2,8,128,128]{4,3,2,1,0:T(8,128)}, u32[]{:S(2)}) copy-start(f32[1,2,8,128,128]{4,3,2,1,0:T(8,128)} %param.3) | copy-start | bytes 3145732
  0.0 18.5 %copy-start = (f32[1,2,8,128,128]{4,3,2,1,0:T(8,128)S(1)}, f32[1,2,8,128,128]{4,3,2,1,0:T(8,128)}, u32[]{:S(2)}) copy-start(f32[1,2,8,128,128]{4,3,2,1,0:T(8,128)} %param.2) | copy-start | bytes 3145732
  0.0 67.2 %collective-permute-start.4 = (f32[2,8,128,128]{3,2,1,0:T(8,128)}, f32[2,8,128,128]{3,2,1,0:T(8,128)S(1)}, u32[]{:S(2)}, u32[]{:S(2)}) collective-permute-start(f32[2,8,128,128]{3,2,1,0:T(8,128)} %bitcast.71), channel_id=1, source_target_pairs={{0,496},{16,0},{32,16},{48,32},{64,48},{80,64},{96,80},{112,96},{1... | collective-permute-start | bytes 3145736 | tf_op jit(solution)/shard_map/ppermute | solution.py:16
  4.0 25.8 %collective-permute-start = (f32[4,1,128,128]{3,2,1,0:T(8,128)S(1)}, f32[4,1,128,128]{3,2,1,0:T(8,128)S(1)}, u32[]{:S(2)}, u32[]{:S(2)}) collective-permute-start(f32[4,1,128,128]{3,2,1,0:T(8,128)S(1)} %get-tuple-element.22), channel_id=1, source_target_pairs={{1,0},{2,1},{3,2},{4,3},{5,4},{6,5},{7,6},{8,7},{9,8},{10,9},{11,1... | collective-permute-start | bytes 786440 | tf_op jit(solution)/shard_map/ppermute | solution.py:27
  16.5 21.4 %collective-permute-start.1 = (f32[4,1,128,128]{3,2,1,0:T(8,128)S(1)}, f32[4,1,128,128]{3,2,1,0:T(8,128)S(1)}, u32[]{:S(2)}, u32[]{:S(2)}) collective-permute-start(f32[4,1,128,128]{3,2,1,0:T(8,128)S(1)} %get-tuple-element.23), channel_id=1, source_target_pairs={{0,1},{1,2},{2,3},{3,4},{4,5},{5,6},{6,7},{7,8},{8,9},{9,10},{10,1... | collective-permute-start | bytes 786440 | tf_op jit(solution)/shard_map/ppermute | solution.py:26
  41.5 10.3 %collective-permute-start.2 = (f32[2,1,128,128]{3,2,1,0:T(8,128)S(1)}, f32[2,1,128,128]{3,2,1,0:T(8,128)S(1)}, u32[]{:S(2)}, u32[]{:S(2)}) collective-permute-start(f32[2,1,128,128]{3,2,1,0:T(8,128)S(1)} %get-tuple-element.52), channel_id=1, source_target_pairs={{1,0},{2,1},{3,2},{4,3},{5,4},{6,5},{7,6},{8,7},{9,8},{10,9},{11,1... | collective-permute-start | bytes 393224 | tf_op jit(solution)/shard_map/ppermute | solution.py:27
  48.2 17.3 %collective-permute-start.3 = (f32[2,1,128,128]{3,2,1,0:T(8,128)S(1)}, f32[2,1,128,128]{3,2,1,0:T(8,128)S(1)}, u32[]{:S(2)}, u32[]{:S(2)}) collective-permute-start(f32[2,1,128,128]{3,2,1,0:T(8,128)S(1)} %get-tuple-element.53), channel_id=1, source_target_pairs={{0,1},{1,2},{2,3},{3,4},{4,5},{5,6},{6,7},{7,8},{8,9},{9,10},{10,1... | collective-permute-start | bytes 393224 | tf_op jit(solution)/shard_map/ppermute | solution.py:26
  68.3 91.0 %collective-permute-start.9 = (f32[2,8,128,128]{3,2,1,0:T(8,128)S(1)}, f32[2,8,128,128]{3,2,1,0:T(8,128)S(1)}, u32[]{:S(2)}, u32[]{:S(2)}) collective-permute-start(f32[2,8,128,128]{3,2,1,0:T(8,128)S(1)} %maximum_subtract_fusion), channel_id=1, source_target_pairs={{0,16},{16,32},{32,48},{48,64},{64,80},{80,96},{96,112},{112,128},... | collective-permute-start | bytes 3145736 | tf_op jit(solution)/shard_map/ppermute | solution.py:16
  92.8 31.9 %collective-permute-start.5 = (f32[2,1,128,128]{3,2,1,0:T(8,128)S(1)}, f32[2,1,128,128]{3,2,1,0:T(8,128)S(1)}, u32[]{:S(2)}, u32[]{:S(2)}) collective-permute-start(f32[2,1,128,128]{3,2,1,0:T(8,128)S(1)} %get-tuple-element.42), channel_id=1, source_target_pairs={{1,0},{2,1},{3,2},{4,3},{5,4},{6,5},{7,6},{8,7},{9,8},{10,9},{11,1... | collective-permute-start | bytes 393224 | tf_op jit(solution)/shard_map/ppermute | solution.py:27
  94.7 30.0 %collective-permute-start.6 = (f32[2,1,128,128]{3,2,1,0:T(8,128)S(1)}, f32[2,1,128,128]{3,2,1,0:T(8,128)S(1)}, u32[]{:S(2)}, u32[]{:S(2)}) collective-permute-start(f32[2,1,128,128]{3,2,1,0:T(8,128)S(1)} %get-tuple-element.43), channel_id=1, source_target_pairs={{0,1},{1,2},{2,3},{3,4},{4,5},{5,6},{6,7},{7,8},{8,9},{9,10},{10,1... | collective-permute-start | bytes 393224 | tf_op jit(solution)/shard_map/ppermute | solution.py:26
  126.0 17.9 %collective-permute-start.7 = (f32[2,1,128,128]{3,2,1,0:T(8,128)S(1)}, f32[2,1,128,128]{3,2,1,0:T(8,128)S(1)}, u32[]{:S(2)}, u32[]{:S(2)}) collective-permute-start(f32[2,1,128,128]{3,2,1,0:T(8,128)S(1)} %get-tuple-element.32), channel_id=1, source_target_pairs={{1,0},{2,1},{3,2},{4,3},{5,4},{6,5},{7,6},{8,7},{9,8},{10,9},{11,1... | collective-permute-start | bytes 393224 | tf_op jit(solution)/shard_map/ppermute | solution.py:27
  140.8 17.1 %collective-permute-start.8 = (f32[2,1,128,128]{3,2,1,0:T(8,128)S(1)}, f32[2,1,128,128]{3,2,1,0:T(8,128)S(1)}, u32[]{:S(2)}, u32[]{:S(2)}) collective-permute-start(f32[2,1,128,128]{3,2,1,0:T(8,128)S(1)} %get-tuple-element.33), channel_id=1, source_target_pairs={{0,1},{1,2},{2,3},{3,4},{4,5},{5,6},{6,7},{7,8},{8,9},{9,10},{10,1... | collective-permute-start | bytes 393224 | tf_op jit(solution)/shard_map/ppermute | solution.py:26
where the time goes:
time: 161 us; the launch traced here: 160 us
  waiting for transfers between devices  74.3 us (46%)
  starting transfers between devices  71.5 us (44%)
  other arithmetic  13.3 us (8%)
    ppermute x4, waiting for transfers between devices, padded(): after = lax.ppermute(initial, axis, down)  38.3 us
    ppermute x4, starting transfers between devices, padded(): after = lax.ppermute(initial, axis, down)  36 us
    ppermute x4, waiting for transfers between devices, padded(): before = lax.ppermute(last, axis, up)  36 us
    ppermute x2, starting transfers between devices, from_behind(): return lax.ppermute(value, axis, pairs)  27.3 us
    ppermute x4, starting transfers between devices, padded(): before = lax.ppermute(last, axis, up)  8.17 us
    add x4, other arithmetic, laplacian(): return total + jnp.roll(core_cells, 1, 3) + jnp.roll(core_cells, -1, 3)  5.23 us
  transfers between devices with their start and end apart: 10, of which 7 were waited for; matrix products, arithmetic and copies ran while one was open for 8% of the time, Pallas kernels for 0%

commit v1 on v0

v1 whole, which is shorter than its diff:
```python
import functools

import jax
import jax.numpy as jnp
from jax import lax
from jax.experimental import pallas as pl
from jax.experimental.pallas import tpu as pltpu
from jax.sharding import PartitionSpec as P

diff_substrate = 0.2
diff_catalyst = 0.1
time_step = 0.8
feed_rate = 0.04
kill_rate = 0.06

MESH = pl.DeviceIdType.MESH
ROW = 4


def laplacian(center, below, above):
    rows, columns = center.shape
    total = -6.0 * center + above + below
    total = total + pltpu.roll(center, 1, 0) + pltpu.roll(center, rows - 1, 0)
    return total + pltpu.roll(center, 1, 1) + pltpu.roll(center, columns - 1, 1)


def base_advance(a, b, spread_a, spread_b):
    growth = a * b * b
    next_a = a + time_step * (diff_substrate * spread_a - growth + feed_rate * (1.0 - a))
    next_b = b + time_step * (diff_catalyst * spread_b + growth - (feed_rate + kill_rate) * b)
    return next_a, next_b


def tangent_advance(a, b, p, q, spread_p, spread_q):
    square = b * b
    cross = 2.0 * a * b
    next_p = p + time_step * (diff_substrate * spread_p - (square + feed_rate) * p - cross * q)
    next_q = q + time_step * (
        diff_catalyst * spread_q + square * p + (cross - feed_rate - kill_rate) * q
    )
    return next_p, next_q


def adjoint_advance(a, b, m, n, spread_m, spread_n):
    square = b * b
    cross = 2.0 * a * b
    next_m = m + time_step * (diff_substrate * spread_m - (square + feed_rate) * m + square * n)
    next_n = n + time_step * (
        diff_catalyst * spread_n - cross * m + (cross - feed_rate - kill_rate) * n
    )
    return next_m, next_n


def kernel(state_hbm, direction_hbm, out_hbm, st, dr, mid, lat, res, adj, out, fol, pri,
           load_sem, store_sem, send_sem, recv_sem):
    depth = lat.shape[0]
    t, s = lax.axis_index("tm"), lax.axis_index("space")
    segments, slabs = lax.axis_size("tm"), lax.axis_size("space")
    up, down = (t, lax.rem(s + 1, slabs)), (t, lax.rem(s + slabs - 1, slabs))
    nxt, prv = (lax.rem(t + 1, segments), s), (lax.rem(t + segments - 1, segments), s)
    wraps = lax.rem(t, ROW) == 0

    barrier = pltpu.get_barrier_semaphore()
    for partner in (up, down, nxt, prv):
        pl.semaphore_signal(barrier, inc=1, device_id=partner, device_id_type=MESH)

    loads = []
    for c in range(2):
        loads.append(pltpu.make_async_copy(
            state_hbm.at[0, c], st.at[pl.ds(1, depth), c], load_sem.at[c]))
        loads.append(pltpu.make_async_copy(
            direction_hbm.at[0, c], dr.at[pl.ds(2, depth), c], load_sem.at[2 + c]))
    for copy in loads:
        copy.start()

    def remote(k, source, target, device):
        return pltpu.make_async_remote_copy(
            src_ref=source, dst_ref=target, send_sem=send_sem.at[k], recv_sem=recv_sem.at[k],
            device_id=device, device_id_type=MESH)

    first = [
        remote(0, st.at[depth], st.at[0], up),
        remote(1, dr.at[pl.ds(depth, 2)], dr.at[pl.ds(0, 2)], up),
        remote(2, st.at[1], st.at[depth + 1], down),
        remote(3, dr.at[pl.ds(2, 2)], dr.at[pl.ds(depth + 2, 2)], down),
    ]
    edges = [
        remote(4, dr.at[2], fol.at[0], prv),
        remote(5, dr.at[depth + 1], fol.at[depth - 1], prv),
    ]
    inner = remote(6, dr.at[pl.ds(3, depth - 2)], fol.at[pl.ds(1, depth - 2)], prv)
    second = [
        remote(7, res.at[depth], res.at[0], up),
        remote(8, res.at[1], res.at[depth + 1], down),
    ]
    third = [
        remote(9, adj.at[depth], adj.at[0], up),
        remote(10, adj.at[1], adj.at[depth + 1], down),
    ]
    bulk = remote(11, res.at[pl.ds(1, depth)], pri, nxt)

    def spread(ref, i):
        return tuple(laplacian(ref[i, c], ref[i - 1, c], ref[i + 1, c]) for c in range(2))

    def later_plane(i):
        lat[i, 0], lat[i, 1] = base_advance(st[i + 1, 0], st[i + 1, 1], *spread(st, i + 1))

    def middle_plane(i):
        mid[i + 1, 0], mid[i + 1, 1] = tangent_advance(
            st[i + 1, 0], st[i + 1, 1], dr[i + 2, 0], dr[i + 2, 1], *spread(dr, i + 2))

    def image_plane(i):
        res[i + 1, 0], res[i + 1, 1] = tangent_advance(
            lat[i, 0], lat[i, 1], mid[i + 1, 0], mid[i + 1, 1], *spread(mid, i + 1))

    def residual_plane(i):
        res[i + 1] = res[i + 1] - fol[i]

    def adjoint_plane(i):
        adj[i + 1, 0], adj[i + 1, 1] = adjoint_advance(
            lat[i, 0], lat[i, 1], res[i + 1, 0], res[i + 1, 1], *spread(res, i + 1))

    def pulled_plane(i):
        out[0, i], out[1, i] = adjoint_advance(
            st[i + 1, 0], st[i + 1, 1], adj[i + 1, 0], adj[i + 1, 1], *spread(adj, i + 1))

    def over(start, stop, *steps):
        @pl.loop(start, stop)
        def _(i):
            for step in steps:
                step(i)

    for copy in loads:
        copy.wait()
    over(1, depth - 1, later_plane, middle_plane)

    pl.semaphore_wait(barrier, 4)
    for copy in first + edges:
        copy.start()

    @pl.when(jnp.logical_not(wraps))
    def _():
        inner.start()

    over(2, depth - 2, image_plane)
    for copy in first:
        copy.wait_send()

    @pl.when(wraps)
    def _():
        inner.start()

    for copy in first:
        copy.wait_recv()
    for i in (0, depth - 1):
        later_plane(i)
    for i in (-1, 0, depth - 1, depth):
        middle_plane(i)
    for i in (0, depth - 1):
        image_plane(i)
    for copy in edges:
        copy.wait()
    for i in (0, depth - 1):
        residual_plane(i)
    for copy in second:
        copy.start()
    for i in (1, depth - 2):
        image_plane(i)
    inner.wait()
    over(1, depth - 1, residual_plane)
    for copy in second:
        copy.wait_send()
    bulk.start()
    over(1, depth - 1, adjoint_plane)
    over(2, depth - 2, pulled_plane)
    for copy in second:
        copy.wait_recv()
    for i in (0, depth - 1):
        adjoint_plane(i)
    for copy in third:
        copy.start()
    for i in (1, depth - 2):
        pulled_plane(i)
    for copy in third:
        copy.wait()
    for i in (0, depth - 1):
        pulled_plane(i)
    bulk.wait()

    @pl.loop(0, depth)
    def _(i):
        for c in range(2):
            out[c, i] = out[c, i] - pri[i, c]

    store = pltpu.make_async_copy(out, out_hbm.at[0], store_sem)
    store.start()
    store.wait()


def local(base_states, direction):
    _, parts, depth, rows, columns = base_states.shape

    def planes(count):
        return pltpu.VMEM((count, parts, rows, columns), jnp.float32)

    return pl.pallas_call(
        kernel,
        out_shape=jax.ShapeDtypeStruct(base_states.shape, jnp.float32),
        in_specs=[pl.BlockSpec(memory_space=pl.ANY)] * 2,
        out_specs=pl.BlockSpec(memory_space=pl.ANY),
        scratch_shapes=[
            planes(depth + 2),
            planes(depth + 4),
            planes(depth + 2),
            planes(depth),
            planes(depth + 2),
            planes(depth + 2),
            pltpu.VMEM((parts, depth, rows, columns), jnp.float32),
            planes(depth),
            planes(depth),
            pltpu.SemaphoreType.DMA((4,)),
            pltpu.SemaphoreType.DMA,
            pltpu.SemaphoreType.DMA((12,)),
            pltpu.SemaphoreType.DMA((12,)),
        ],
        compiler_params=pltpu.CompilerParams(
            collective_id=0, has_side_effects=True, vmem_limit_bytes=40 * 2**20
        ),
    )(base_states, direction)


def solution(mesh):
    spec = P("tm", None, "space", None, None)
    return jax.shard_map(
        local, mesh=mesh, in_specs=(spec, spec), out_specs=spec, check_vma=False
    )
```

time: 161 us -> 117 us (0.73)
  the two profiles are of different devices: /device:TPU:134 before, /device:TPU:1 now
where the time goes in v1:
time: 117 us; the launch traced here: 116 us
  Pallas kernels  113 us (97%)
  local copies, waits for them, and re-layouts  3.42 us (3%)
    pallas_call x1, Pallas kernels, local(): pl.pallas_call(kernel, out_shape=jax.ShapeDtypeStruct(base_states.shape,...  113 us
    unnamed x5, local copies, waits for them, and re-layouts  3.42 us

profile of v1, /device:TPU:1, one launch (start us, length us, event | category | flops | bytes accessed | tf_op | source)
XLA Modules:
  0.0 116.4 jit_solution(17033986216097875752)
XLA Ops:
  0.0 0.0 copy-start
  0.0 1.2 %copy-done = f32[1,2,8,128,128]{4,3,2,1,0:T(8,128)S(1)} copy-done((f32[1,2,8,128,128]{4,3,2,1,0:T(8,128)S(1)}, f32[1,2,8,128,128]{4,3,2,1,0:T(8,128)}, u32[]{:S(2)}) %copy-start) | copy-done | bytes 1048600
  1.2 0.0 copy-start.1
  1.2 1.2 %copy-done.1 = f32[1,2,8,128,128]{4,3,2,1,0:T(8,128)S(1)} copy-done((f32[1,2,8,128,128]{4,3,2,1,0:T(8,128)S(1)}, f32[1,2,8,128,128]{4,3,2,1,0:T(8,128)}, u32[]{:S(2)}) %copy-start.1) | copy-done | bytes 1048600
  2.5 113.0 %shard_map.28 = f32[1,2,8,128,128]{4,3,2,1,0:T(8,128)S(1)} custom-call(f32[1,2,8,128,128]{4,3,2,1,0:T(8,128)S(1)} %copy-done, f32[1,2,8,128,128]{4,3,2,1,0:T(8,128)S(1)} %copy-done.1), custom_call_target="tpu_custom_call" | custom-call | tf_op jit(solution)/shard_map/pallas_call | solution.py:206
  115.4 1.0 copy.4
Async XLA Ops:
  0.0 1.2 %copy-start = (f32[1,2,8,128,128]{4,3,2,1,0:T(8,128)S(1)}, f32[1,2,8,128,128]{4,3,2,1,0:T(8,128)}, u32[]{:S(2)}) copy-start(f32[1,2,8,128,128]{4,3,2,1,0:T(8,128)} %state_hbm.1) | copy-start | bytes 3145732
  1.2 1.2 %copy-start.1 = (f32[1,2,8,128,128]{4,3,2,1,0:T(8,128)S(1)}, f32[1,2,8,128,128]{4,3,2,1,0:T(8,128)}, u32[]{:S(2)}) copy-start(f32[1,2,8,128,128]{4,3,2,1,0:T(8,128)} %direction_hbm.1) | copy-start | bytes 3145732

commit v2 on v1

--- a/solution.py
+++ b/solution.py
@@ -51,18 +51,46 @@
     return next_m, next_n
 
 
-def kernel(state_hbm, direction_hbm, out_hbm, st, dr, mid, lat, res, adj, out, fol, pri,
-           load_sem, store_sem, send_sem, recv_sem):
+def kernel(state_hbm, direction_hbm, out_hbm, st, dr, mid, lat, res, adj, out, fol, pri, dr_pass,
+           res_pass, load_sem, store_sem, send_sem, recv_sem):
     depth = lat.shape[0]
     t, s = lax.axis_index("tm"), lax.axis_index("space")
     segments, slabs = lax.axis_size("tm"), lax.axis_size("space")
+    x = lax.rem(t, ROW)
+    first_x, last_x = x == 0, x == ROW - 1
+    other_x = jnp.logical_not(jnp.logical_or(first_x, last_x))
+
+    def at(steps):
+        return (lax.rem(t + steps + segments, segments), s)
+
     up, down = (t, lax.rem(s + 1, slabs)), (t, lax.rem(s + slabs - 1, slabs))
-    nxt, prv = (lax.rem(t + 1, segments), s), (lax.rem(t + segments - 1, segments), s)
-    wraps = lax.rem(t, ROW) == 0
+    nxt, prv = at(1), at(-1)
+
+    def when(condition, *copies):
+        @pl.when(condition)
+        def _():
+            for copy in copies:
+                copy.start()
 
     barrier = pltpu.get_barrier_semaphore()
-    for partner in (up, down, nxt, prv):
-        pl.semaphore_signal(barrier, inc=1, device_id=partner, device_id_type=MESH)
+
+    def greet(*partners):
+        for partner in partners:
+            pl.semaphore_signal(barrier, inc=1, device_id=partner, device_id_type=MESH)
+
+    greet(up, down, nxt, prv)
+
+    @pl.when(first_x)
+    def _():
+        greet(at(ROW - 1), *(at(r - ROW) for r in range(ROW - 1)))
+
+    @pl.when(last_x)
+    def _():
+        greet(at(1 - ROW), *(at(r + 1) for r in range(1, ROW)))
+
+    @pl.when(other_x)
+    def _():
+        greet(at(-x), at(ROW - 1 - x))
 
     loads = []
     for c in range(2):
@@ -73,31 +101,53 @@
     for copy in loads:
         copy.start()
 
-    def remote(k, source, target, device):
+    def remote(source, target, device, sent, received):
         return pltpu.make_async_remote_copy(
-            src_ref=source, dst_ref=target, send_sem=send_sem.at[k], recv_sem=recv_sem.at[k],
-            device_id=device, device_id_type=MESH)
+            src_ref=source, dst_ref=target, send_sem=send_sem.at[sent],
+            recv_sem=recv_sem.at[received], device_id=device, device_id_type=MESH)
 
     first = [
-        remote(0, st.at[depth], st.at[0], up),
-        remote(1, dr.at[pl.ds(depth, 2)], dr.at[pl.ds(0, 2)], up),
-        remote(2, st.at[1], st.at[depth + 1], down),
-        remote(3, dr.at[pl.ds(2, 2)], dr.at[pl.ds(depth + 2, 2)], down),
+        remote(st.at[depth], st.at[0], up, 0, 0),
+        remote(dr.at[pl.ds(depth, 2)], dr.at[pl.ds(0, 2)], up, 1, 1),
+        remote(st.at[1], st.at[depth + 1], down, 2, 2),
+        remote(dr.at[pl.ds(2, 2)], dr.at[pl.ds(depth + 2, 2)], down, 3, 3),
+    ]
+    second = [
+        remote(res.at[depth], res.at[0], up, 4, 4),
+        remote(res.at[1], res.at[depth + 1], down, 5, 5),
+    ]
+    third = [
+        remote(adj.at[depth], adj.at[0], up, 6, 6),
+        remote(adj.at[1], adj.at[depth + 1], down, 7, 7),
     ]
     edges = [
-        remote(4, dr.at[2], fol.at[0], prv),
-        remote(5, dr.at[depth + 1], fol.at[depth - 1], prv),
-    ]
-    inner = remote(6, dr.at[pl.ds(3, depth - 2)], fol.at[pl.ds(1, depth - 2)], prv)
-    second = [
-        remote(7, res.at[depth], res.at[0], up),
-        remote(8, res.at[1], res.at[depth + 1], down),
-    ]
-    third = [
-        remote(9, adj.at[depth], adj.at[0], up),
-        remote(10, adj.at[1], adj.at[depth + 1], down),
-    ]
-    bulk = remote(11, res.at[pl.ds(1, depth)], pri, nxt)
+        remote(dr.at[2], fol.at[0], prv, 8, 8),
+        remote(dr.at[depth + 1], fol.at[depth - 1], prv, 9, 9),
+    ]
+
+    def part(r):
+        return pl.ds(2 * r - 1, 2)
+
+    inner = [
+        remote(dr.at[pl.ds(2 * r + 1, 2)], fol.at[part(r)], prv, 9 + r, 9 + r)
+        for r in range(1, ROW)
+    ]
+    inner_by = [
+        remote(dr.at[pl.ds(2 * r + 1, 2)], dr_pass, at(r), 9 + r, 13) for r in range(1, ROW)
+    ]
+    inner_on = [remote(dr_pass, fol.at[part(r)], at(-1 - r), 13, 9 + r) for r in range(1, ROW)]
+    bulk = [
+        remote(res.at[pl.ds(2 * r + 1, 2)], pri.at[pl.ds(2 * r, 2)], nxt, 14 + r, 14 + r)
+        for r in range(ROW)
+    ]
+    bulk_by = [
+        remote(res.at[pl.ds(2 * r + 1, 2)], res_pass, at(r + 1 - ROW), 14 + r, 18)
+        for r in range(ROW - 1)
+    ]
+    bulk_on = [
+        remote(res_pass, pri.at[pl.ds(2 * r, 2)], at(ROW - r), 18, 14 + r)
+        for r in range(ROW - 1)
+    ]
 
     def spread(ref, i):
         return tuple(laplacian(ref[i, c], ref[i - 1, c], ref[i + 1, c]) for c in range(2))
@@ -134,58 +184,66 @@
         copy.wait()
     over(1, depth - 1, later_plane, middle_plane)
 
-    pl.semaphore_wait(barrier, 4)
-    for copy in first + edges:
+    @pl.when(other_x)
+    def _():
+        pl.semaphore_wait(barrier, 6)
+
+    @pl.when(jnp.logical_not(other_x))
+    def _():
+        pl.semaphore_wait(barrier, 8)
+
+    for copy in first:
         copy.start()
-
-    @pl.when(jnp.logical_not(wraps))
-    def _():
-        inner.start()
-
+    when(jnp.logical_not(first_x), *edges, *inner)
+    when(first_x, *inner_by)
     over(2, depth - 2, image_plane)
     for copy in first:
         copy.wait_send()
-
-    @pl.when(wraps)
-    def _():
-        inner.start()
-
-    for copy in first:
-        copy.wait_recv()
-    for i in (0, depth - 1):
-        later_plane(i)
-    for i in (-1, 0, depth - 1, depth):
-        middle_plane(i)
-    for i in (0, depth - 1):
-        image_plane(i)
-    for copy in edges:
-        copy.wait()
-    for i in (0, depth - 1):
-        residual_plane(i)
-    for copy in second:
-        copy.start()
+    when(first_x, *edges)
+    for r in range(1, ROW):
+        @pl.when(x == r)
+        def _(r=r):
+            inner_by[r - 1].wait_recv()
+            inner_on[r - 1].start()
+
+    for side, end in ((0, 0), (1, depth - 1)):
+        for copy in first[2 * side:2 * side + 2]:
+            copy.wait_recv()
+        later_plane(end)
+        middle_plane(end)
+        middle_plane(end + 2 * side - 1)
+        image_plane(end)
+        edges[side].wait()
+        residual_plane(end)
+        second[1 - side].start()
     for i in (1, depth - 2):
         image_plane(i)
-    inner.wait()
+    for copy in inner:
+        copy.wait()
     over(1, depth - 1, residual_plane)
+    when(jnp.logical_not(last_x), *bulk)
+    when(last_x, *bulk_by)
     for copy in second:
         copy.wait_send()
-    bulk.start()
+    when(last_x, bulk[ROW - 1])
     over(1, depth - 1, adjoint_plane)
+    for r in range(ROW - 1):
+        @pl.when(x == r)
+        def _(r=r):
+            bulk_by[r].wait_recv()
+            bulk_on[r].start()
     over(2, depth - 2, pulled_plane)
-    for copy in second:
-        copy.wait_recv()
-    for i in (0, depth - 1):
-        adjoint_plane(i)
-    for copy in third:
-        copy.start()
+    for side, end in ((0, 0), (1, depth - 1)):
+        second[side].wait_recv()
+        adjoint_plane(end)
+        third[1 - side].start()
     for i in (1, depth - 2):
         pulled_plane(i)
-    for copy in third:
+    for side, end in ((0, 0), (1, depth - 1)):
+        third[side].wait_recv()
+        pulled_plane(end)
+    for copy in bulk:
         copy.wait()
-    for i in (0, depth - 1):
-        pulled_plane(i)
-    bulk.wait()
 
     @pl.loop(0, depth)
     def _(i):
@@ -194,6 +252,17 @@
 
     store = pltpu.make_async_copy(out, out_hbm.at[0], store_sem)
     store.start()
+    for copy in third:
+        copy.wait_send()
+
+    @pl.when(jnp.logical_not(first_x))
+    def _():
+        inner_on[0].wait_send()
+
+    @pl.when(jnp.logical_not(last_x))
+    def _():
+        bulk_on[0].wait_send()
+
     store.wait()
 
 
@@ -218,10 +287,12 @@
             pltpu.VMEM((parts, depth, rows, columns), jnp.float32),
             planes(depth),
             planes(depth),
+            planes(2),
+            planes(2),
             pltpu.SemaphoreType.DMA((4,)),
             pltpu.SemaphoreType.DMA,
-            pltpu.SemaphoreType.DMA((12,)),
-            pltpu.SemaphoreType.DMA((12,)),
+            pltpu.SemaphoreType.DMA((19,)),
+            pltpu.SemaphoreType.DMA((19,)),
         ],
         compiler_params=pltpu.CompilerParams(
             collective_id=0, has_side_effects=True, vmem_limit_bytes=40 * 2**20

time: 117 us -> 101 us (0.86)
  the two profiles are of different devices: /device:TPU:1 before, /device:TPU:16 now
where the time goes in v2:
time: 101 us
  Pallas kernels  97.2 us (96%)
  local copies, waits for them, and re-layouts  3.42 us (3%)
    pallas_call x1, Pallas kernels, local(): pl.pallas_call(kernel, out_shape=jax.ShapeDtypeStruct(base_states.shape,...  97.2 us
    unnamed x5, local copies, waits for them, and re-layouts  3.42 us

profile of v2, /device:TPU:16, one launch (start us, length us, event | category | flops | bytes accessed | tf_op | source)
XLA Modules:
  0.0 100.6 jit_solution(10074181682791944370)
XLA Ops:
  0.0 0.0 copy-start
  0.0 1.2 %copy-done = f32[1,2,8,128,128]{4,3,2,1,0:T(8,128)S(1)} copy-done((f32[1,2,8,128,128]{4,3,2,1,0:T(8,128)S(1)}, f32[1,2,8,128,128]{4,3,2,1,0:T(8,128)}, u32[]{:S(2)}) %copy-start) | copy-done | bytes 1048600
  1.2 0.0 copy-start.1
  1.2 1.2 %copy-done.1 = f32[1,2,8,128,128]{4,3,2,1,0:T(8,128)S(1)} copy-done((f32[1,2,8,128,128]{4,3,2,1,0:T(8,128)S(1)}, f32[1,2,8,128,128]{4,3,2,1,0:T(8,128)}, u32[]{:S(2)}) %copy-start.1) | copy-done | bytes 1048600
  2.5 97.2 %shard_map.28 = f32[1,2,8,128,128]{4,3,2,1,0:T(8,128)S(1)} custom-call(f32[1,2,8,128,128]{4,3,2,1,0:T(8,128)S(1)} %copy-done, f32[1,2,8,128,128]{4,3,2,1,0:T(8,128)S(1)} %copy-done.1), custom_call_target="tpu_custom_call" | custom-call | tf_op jit(solution)/shard_map/pallas_call | solution.py:275
  99.6 1.0 copy.4
Async XLA Ops:
  0.0 1.2 %copy-start = (f32[1,2,8,128,128]{4,3,2,1,0:T(8,128)S(1)}, f32[1,2,8,128,128]{4,3,2,1,0:T(8,128)}, u32[]{:S(2)}) copy-start(f32[1,2,8,128,128]{4,3,2,1,0:T(8,128)} %state_hbm.1) | copy-start | bytes 3145732
  1.2 1.2 %copy-start.1 = (f32[1,2,8,128,128]{4,3,2,1,0:T(8,128)S(1)}, f32[1,2,8,128,128]{4,3,2,1,0:T(8,128)}, u32[]{:S(2)}) copy-start(f32[1,2,8,128,128]{4,3,2,1,0:T(8,128)} %direction_hbm.1) | copy-start | bytes 3145732

commit v3 on v2

v3 whole, which is shorter than its diff:
```python
import functools

import jax
import jax.numpy as jnp
from jax import lax
from jax.experimental import pallas as pl
from jax.experimental.pallas import tpu as pltpu
from jax.sharding import PartitionSpec as P

diff_substrate = 0.2
diff_catalyst = 0.1
time_step = 0.8
feed_rate = 0.04
kill_rate = 0.06

MESH = pl.DeviceIdType.MESH
ROW = 4
COPIES = 60
EARLY = 0
LOTS = 8
WINDOW = 4
PACED = 3
FOLLOW = (-1, 1, 1, 1)
PRIOR = (0, 0, 0, 0)
BY_FIRST = False
TILE = 8


def pieces(region, rows):
    start, count = region
    start = start % rows
    ahead = min(count, rows - start)
    spans = [(start, ahead)]
    if count > ahead:
        spans.append((0, count - ahead))
    return spans


def take(plane, region):
    spans = pieces(region, plane.shape[0])
    if len(spans) == 1 and spans[0][1] == plane.shape[0]:
        return plane[...]
    values = [plane[pl.ds(start, count)] for start, count in spans]
    return values[0] if len(values) == 1 else jnp.concatenate(values, axis=0)


def put(plane, region, value):
    done = 0
    for start, count in pieces(region, plane.shape[0]):
        plane[pl.ds(start, count)] = value[done:done + count]
        done += count


def laplacian(center, below, above, region):
    rows, columns = center.shape
    start, count = region
    cells = take(center, region)
    total = -6.0 * cells + take(above, region) + take(below, region)
    if count == rows:
        total = total + pltpu.roll(cells, 1, 0) + pltpu.roll(cells, rows - 1, 0)
    else:
        length = count + 2 * TILE
        wide = take(center, (start - TILE, length))
        inside = slice(TILE, TILE + count)
        total = total + pltpu.roll(wide, 1, 0)[inside] + pltpu.roll(wide, length - 1, 0)[inside]
    return total + pltpu.roll(cells, 1, 1) + pltpu.roll(cells, columns - 1, 1)


def base_advance(a, b, spread_a, spread_b):
    growth = a * b * b
    next_a = a + time_step * (diff_substrate * spread_a - growth + feed_rate * (1.0 - a))
    next_b = b + time_step * (diff_catalyst * spread_b + growth - (feed_rate + kill_rate) * b)
    return next_a, next_b


def tangent_advance(a, b, p, q, spread_p, spread_q):
    square = b * b
    cross = 2.0 * a * b
    next_p = p + time_step * (diff_substrate * spread_p - (square + feed_rate) * p - cross * q)
    next_q = q + time_step * (
        diff_catalyst * spread_q + square * p + (cross - feed_rate - kill_rate) * q
    )
    return next_p, next_q


def adjoint_advance(a, b, m, n, spread_m, spread_n):
    square = b * b
    cross = 2.0 * a * b
    next_m = m + time_step * (diff_substrate * spread_m - (square + feed_rate) * m + square * n)
    next_n = n + time_step * (
        diff_catalyst * spread_n - cross * m + (cross - feed_rate - kill_rate) * n
    )
    return next_m, next_n


def kernel(early, state_hbm, direction_hbm, out, st, dr, mid, lat, res, adj, fol, pri,
           dr_pass, res_pass, load_sem, send_sem, recv_sem):
    depth, rows = lat.shape[0], lat.shape[2]
    t, s = lax.axis_index("tm"), lax.axis_index("space")
    segments, slabs = lax.axis_size("tm"), lax.axis_size("space")
    x = lax.rem(t, ROW)
    first_x, last_x = x == 0, x == ROW - 1
    other_x = jnp.logical_not(jnp.logical_or(first_x, last_x))

    def at(steps):
        return (lax.rem(t + steps + segments, segments), s)

    up, down = (t, lax.rem(s + 1, slabs)), (t, lax.rem(s + slabs - 1, slabs))
    nxt, prv = at(1), at(-1)

    whole = (0, rows)
    group = [
        ((start, early - 2 * start), (early - start, rows - early + 2 * start))
        if early else (None, whole)
        for start in (0, TILE, 2 * TILE)
    ]

    def when(condition, *copies):
        @pl.when(condition)
        def _():
            for copy in copies:
                copy.start()

    barrier = pltpu.get_barrier_semaphore()

    def greet(*partners):
        for partner in partners:
            pl.semaphore_signal(barrier, inc=1, device_id=partner, device_id_type=MESH)

    greet(up, down, nxt, prv)

    @pl.when(first_x)
    def _():
        greet(at(ROW - 1), *(at(r - ROW) for r in range(ROW - 1)))

    @pl.when(last_x)
    def _():
        greet(at(1 - ROW), *(at(r + 1) for r in range(1, ROW)))

    @pl.when(other_x)
    def _():
        greet(at(-x), at(ROW - 1 - x))

    loads = []
    for c in range(2):
        loads.append(pltpu.make_async_copy(
            state_hbm.at[0, c], st.at[pl.ds(1, depth), c], load_sem.at[c]))
        loads.append(pltpu.make_async_copy(
            direction_hbm.at[0, c], dr.at[pl.ds(2, depth), c], load_sem.at[2 + c]))
    for copy in loads:
        copy.start()

    def remote(source, target, device, sent, received):
        return pltpu.make_async_remote_copy(
            src_ref=source, dst_ref=target, send_sem=send_sem.at[sent],
            recv_sem=recv_sem.at[received], device_id=device, device_id_type=MESH)

    used = [0]

    def halo(ref, region, count):
        ghosts = (ref.shape[0] - depth) // 2
        spans = pieces(region, rows) if region else []
        sides = []
        for source, target, device in (
            (depth + ghosts - count, ghosts - count, up), (ghosts, depth + ghosts, down)
        ):
            copies = []
            for start, length in spans:
                k = used[0]
                used[0] += 1
                copies.append(remote(
                    ref.at[pl.ds(source, count), :, pl.ds(start, length)],
                    ref.at[pl.ds(target, count), :, pl.ds(start, length)], device, k, k))
            sides.append(copies)
        return sides

    lots = [[p + q for p, q in zip(halo(st, (i * rows // LOTS, rows // LOTS), 1), halo(dr, (i * rows // LOTS, rows // LOTS), 2))] for i in range(LOTS)]
    paced = t >= PACED * ROW
    free = jnp.logical_not(paced)

    halos = [
        [[[], []], [sum((lot[side] for lot in lots), []) for side in range(2)]],
        [halo(res, region, 1) for region in group[1]],
        [halo(adj, region, 1) for region in group[2]],
    ]

    def send(copies):
        for side in copies:
            for copy in side:
                copy.start()

    def sent(copies):
        for side in copies:
            for copy in side:
                copy.wait_send()

    def arrived(copies):
        for copy in copies:
            copy.wait_recv()

    base = used[0]
    edges = [remote(dr.at[i + 2], fol.at[i], prv, base + k, base + k)
             for k, i in enumerate((0, depth - 1))]
    base = base + 2
    follow, follow_by, follow_on = [], [], []
    for r in range(ROW - 1):
        source, target = dr.at[pl.ds(2 * r + 3, 2)], fol.at[pl.ds(2 * r + 1, 2)]
        follow.append(remote(source, target, prv, base + r, base + r))
        follow_by.append(remote(source, dr_pass, at(r + 1), base + r, base + 3))
        follow_on.append(remote(dr_pass, target, at(-2 - r), base + 3, base + r))
    base = base + 4
    prior, prior_by, prior_on = [], [], []
    for r in range(ROW):
        source, target = res.at[pl.ds(2 * r + 1, 2)], pri.at[pl.ds(2 * r, 2)]
        prior.append(remote(source, target, nxt, base + r, base + r))
        prior_by.append(remote(source, res_pass, at(r + 1 - ROW), base + r, base + 4))
        prior_on.append(remote(res_pass, target, at(ROW - r), base + 4, base + r))

    def relay(r, coming, going):
        @pl.when(x == r)
        def _():
            coming.wait_recv()
            going.start()

    def spread(ref, i, region):
        return tuple(
            laplacian(ref.at[i, c], ref.at[i - 1, c], ref.at[i + 1, c], region) for c in range(2))

    def pair(ref, i, region):
        return tuple(take(ref.at[i, c], region) for c in range(2))

    def keep(ref, i, region, values):
        for c in range(2):
            put(ref.at[i, c], region, values[c])

    def later_plane(i, region=whole):
        keep(lat, i, region, base_advance(*pair(st, i + 1, region), *spread(st, i + 1, region)))

    def middle_plane(i, region=whole):
        keep(mid, i + 1, region, tangent_advance(
            *pair(st, i + 1, region), *pair(dr, i + 2, region), *spread(dr, i + 2, region)))

    def image_plane(i, region=whole):
        keep(res, i + 1, region, tangent_advance(
            *pair(lat, i, region), *pair(mid, i + 1, region), *spread(mid, i + 1, region)))

    def residual_plane(i, region=whole):
        keep(res, i + 1, region, tuple(
            value - other for value, other in zip(pair(res, i + 1, region), pair(fol, i, region))))

    def adjoint_plane(i, region=whole):
        keep(adj, i + 1, region, adjoint_advance(
            *pair(lat, i, region), *pair(res, i + 1, region), *spread(res, i + 1, region)))

    def pulled_plane(i):
        values = adjoint_advance(
            *pair(st, i + 1, whole), *pair(adj, i + 1, whole), *spread(adj, i + 1, whole))
        for c in range(2):
            out[0, c, i] = values[c]

    def product_plane(i):
        for c in range(2):
            out[0, c, i] = out[0, c, i] - pri[i, c]

    def over(start, stop, *steps):
        @pl.loop(start, stop)
        def _(i):
            for step in steps:
                step(i)

    sides = ((0, 0, -1), (1, depth - 1, depth))

    def follow_event(now):
        if FOLLOW[0] == now:
            when(first_x, *edges)
        for r in range(ROW - 1):
            if FOLLOW[r + 1] == now:
                relay(r + 1, follow_by[r], follow_on[r])

    def prior_event(now):
        if PRIOR[ROW - 1] == now:
            when(last_x, prior[ROW - 1])
        for r in range(ROW - 1):
            if PRIOR[r] == now:
                relay(r, prior_by[r], prior_on[r])

    for copy in loads:
        copy.wait()
    over(1, depth - 1, later_plane, middle_plane)

    @pl.when(other_x)
    def _():
        pl.semaphore_wait(barrier, 6)

    @pl.when(jnp.logical_not(other_x))
    def _():
        pl.semaphore_wait(barrier, 8)

    follow_event(-1)
    if BY_FIRST:
        when(first_x, *follow_by)
    for lot in lots[:WINDOW]:
        send(lot)
    for lot in lots[WINDOW:]:
        when(free, *lot[0], *lot[1])
    if not BY_FIRST:
        when(first_x, *follow_by)
    when(jnp.logical_not(first_x), *edges, *follow)
    follow_event(0)
    over(2, depth - 2, image_plane)
    follow_event(1)

    @pl.when(paced)
    def _():
        for i in range(WINDOW, LOTS):
            for side in range(2):
                arrived(lots[i - WINDOW][side])
            send(lots[i])


    def first_round(half):
        for side, end, ghost in sides:
            @pl.when(free)
            def _(side=side):
                for lot in lots[:LOTS - WINDOW]:
                    arrived(lot[side])

            for lot in lots[LOTS - WINDOW:]:
                arrived(lot[side])
            later_plane(end, group[0][half])
            middle_plane(end, group[0][half])
            middle_plane(ghost, group[1][half])
            image_plane(end, group[1][half])
            if not half or not early:
                edges[side].wait_recv()
            residual_plane(end, group[1][half])
            for copy in halos[1][half][1 - side]:
                copy.start()

    def second_round(half):
        for side, end, _ in sides:
            arrived(halos[1][half][side])
            adjoint_plane(end, group[2][half])
            for copy in halos[2][half][1 - side]:
                copy.start()

    if early:
        sent(halos[0][0])
        follow_event(2)
        send(halos[0][1])
        follow_event(3)
        first_round(0)
    sent(halos[0][1])
    follow_event(4)
    first_round(1)
    for i in (1, depth - 2):
        image_plane(i)
    for copy in follow:
        copy.wait_recv()
    over(1, depth - 1, residual_plane)
    when(jnp.logical_not(last_x), *prior)
    when(last_x, *prior_by[:ROW - 1])
    prior_event(0)
    if early:
        second_round(0)
    prior_event(1)
    over(1, depth - 1, adjoint_plane)
    sent(halos[1][0])
    sent(halos[1][1])
    prior_event(2)
    over(2, depth - 2, pulled_plane)
    second_round(1)
    for i in (1, depth - 2):
        pulled_plane(i)
    prior_event(3)
    sent(halos[2][0])
    sent(halos[2][1])
    prior_event(4)
    for side, end, _ in sides:
        arrived(halos[2][0][side])
        arrived(halos[2][1][side])
        pulled_plane(end)
    for copy in prior:
        copy.wait_recv()
    over(0, depth, product_plane)
    for copy in edges + follow + prior:
        copy.wait_send()

    @pl.when(jnp.logical_not(first_x))
    def _():
        follow_on[0].wait_send()

    @pl.when(jnp.logical_not(last_x))
    def _():
        prior_on[0].wait_send()


def local(base_states, direction):
    _, parts, depth, rows, columns = base_states.shape

    def planes(count):
        return pltpu.VMEM((count, parts, rows, columns), jnp.float32)

    return pl.pallas_call(
        functools.partial(kernel, rows * EARLY // 16),
        out_shape=jax.ShapeDtypeStruct(base_states.shape, jnp.float32),
        in_specs=[pl.BlockSpec(memory_space=pl.ANY)] * 2,
        out_specs=pl.BlockSpec(memory_space=pltpu.VMEM),
        scratch_shapes=[
            planes(depth + 2),
            planes(depth + 4),
            planes(depth + 2),
            planes(depth),
            planes(depth + 2),
            planes(depth + 2),
            planes(depth),
            planes(depth),
            planes(2),
            planes(2),
            pltpu.SemaphoreType.DMA((4,)),
            pltpu.SemaphoreType.DMA((COPIES,)),
            pltpu.SemaphoreType.DMA((COPIES,)),
        ],
        compiler_params=pltpu.CompilerParams(
            collective_id=0, has_side_effects=True, vmem_limit_bytes=40 * 2**20
        ),
    )(*(pltpu.with_memory_space_constraint(x, pltpu.HBM) for x in (base_states, direction)))


def solution(mesh):
    spec = P("tm", None, "space", None, None)
    return jax.shard_map(
        local, mesh=mesh, in_specs=(spec, spec), out_specs=spec, check_vma=False
    )
```

time: 101 us -> 97.8 us (0.968)
  the two profiles are of different devices: /device:TPU:16 before, /device:TPU:1 now
where the time goes in v3:
time: 97.8 us; the launch traced here: 96 us
  Pallas kernels  95 us (97%)
    pallas_call x1, Pallas kernels, local(): pl.pallas_call(functools.partial(kernel, rows * EARLY // 16), out_shape=j...  95 us

profile of v3, /device:TPU:1, one launch (start us, length us, event | category | flops | bytes accessed | tf_op | source)
XLA Modules:
  0.0 96.0 jit_solution(6673860890676908253)
XLA Ops:
  0.0 95.0 %shard_map.28 = f32[1,2,8,128,128]{4,3,2,1,0:T(8,128)S(1)} custom-call(f32[1,2,8,128,128]{4,3,2,1,0:T(8,128)} %state_hbm.1, f32[1,2,8,128,128]{4,3,2,1,0:T(8,128)} %direction_hbm.1), custom_call_target="tpu_custom_call" | custom-call | tf_op jit(solution)/shard_map/pallas_call | solution.py:404
  95.0 1.0 %copy.4 = f32[1,2,8,128,128]{4,3,2,1,0:T(8,128)} copy(f32[1,2,8,128,128]{4,3,2,1,0:T(8,128)S(1)} %shard_map.28) | data formatting | bytes 2097152

commit v4 on v3

--- a/solution.py
+++ b/solution.py
@@ -376,13 +376,14 @@
     sent(halos[2][0])
     sent(halos[2][1])
     prior_event(4)
+    for copy in prior:
+        copy.wait_recv()
+    over(1, depth - 1, product_plane)
     for side, end, _ in sides:
         arrived(halos[2][0][side])
         arrived(halos[2][1][side])
         pulled_plane(end)
-    for copy in prior:
-        copy.wait_recv()
-    over(0, depth, product_plane)
+        product_plane(end)
     for copy in edges + follow + prior:
         copy.wait_send()
 

time: 97.8 us -> 97.7 us (level)
  no operation moved by 1% of the time
where the time goes in v4:
time: 97.7 us; the launch traced here: 96.2 us
  Pallas kernels  95.2 us (97%)
    pallas_call x1, Pallas kernels, local(): pl.pallas_call(functools.partial(kernel, rows * EARLY // 16), out_shape=j...  95.2 us

profile of v4, /device:TPU:1, one launch (start us, length us, event | category | flops | bytes accessed | tf_op | source)
XLA Modules:
  0.0 96.2 jit_solution(7937820347452284932)
XLA Ops:
  0.0 95.2 %shard_map.28 = f32[1,2,8,128,128]{4,3,2,1,0:T(8,128)S(1)} custom-call(f32[1,2,8,128,128]{4,3,2,1,0:T(8,128)} %state_hbm.1, f32[1,2,8,128,128]{4,3,2,1,0:T(8,128)} %direction_hbm.1), custom_call_target="tpu_custom_call" | custom-call | tf_op jit(solution)/shard_map/pallas_call | solution.py:405
  95.2 1.0 %copy.4 = f32[1,2,8,128,128]{4,3,2,1,0:T(8,128)} copy(f32[1,2,8,128,128]{4,3,2,1,0:T(8,128)S(1)} %shard_map.28) | data formatting | bytes 2097152
